TPU v7x, 512 devices: a whole 4x8x8 slice. The times are simulated.
512 devices in a mesh: tile: 128 (over z, y, core), panel: 4 (over x).
Axes of the slice: x: 4, y: 8, z: 8, core: 2. Of those that a mesh axis runs over, the one named last changes fastest.
Arguments:
- reconstructor: bfloat16 [128, 30720], P('panel', 'tile'), may hold values from -6 to 6
- c_as: bfloat16 [128, 30720], P('panel', 'tile'), may hold values from -6 to 6
- tiles: bfloat16 [128, 2048, 2048], P('tile', 'panel'), may hold values from -0.03125 to 0.03125
- tile_pairs: int32 [120, 2], replicated, may hold values from 0 to 14, as said below
- tile_slot: int32 [120], replicated, may hold values from 0 to 127, as said below
Outputs:
- grad_out: float32 [128, 30720], P('panel', 'tile')
Inputs may be any that keep to these rules, and one draw needn't show every extreme that they name: `tile_pairs`: each pair (a, b) with b <= a < 15 appears exactly once. `tile_slot`: distinct slots; slot s belongs to index s // 1 of tile; each index of tile holds one slot; 120 of the 128 slots are used, slots 0 and 127 always among them.
All inputs are finite; a program needn't handle non-finite values.
Results may differ from a plain program's by a relative error of at most 0.0003.
Values may be sent and summed in bfloat16 or wider, within the bound.
A program may use at most 64 MiB of HBM per device.

v0:
```python
import jax
import jax.numpy as jnp
from jax import lax
from jax.sharding import PartitionSpec as P


def add_into(running, contrib, column_start):
    current = lax.dynamic_slice_in_dim(running, column_start, contrib.shape[1], 1)
    return lax.dynamic_update_slice_in_dim(running, current + contrib, column_start, 1)


def body(reconstructor, c_as, tiles, tile_pairs, tile_slot):
    whole_rows = lax.all_gather(reconstructor, "tile", axis=1, tiled=True)
    act_rows = whole_rows.shape[0]
    slope_count = whole_rows.shape[1]
    slot_count = tiles.shape[0]
    tile_size = tiles.shape[2]
    first_slot = lax.axis_index("tile") * slot_count
    local_slots = first_slot + jnp.arange(slot_count, dtype=jnp.int32)
    matches = tile_slot[:, None] == local_slots[None, :]
    is_live = jnp.any(matches, axis=0)
    lower_blocks = jnp.sum(jnp.where(matches, tile_pairs[:, 0:1], 0), axis=0)
    upper_blocks = jnp.sum(jnp.where(matches, tile_pairs[:, 1:2], 0), axis=0)
    factors = jnp.where(is_live, jnp.where(lower_blocks == upper_blocks, 0.5, 1.0), 0.0).astype(
        jnp.float32
    )
    tile_piece = lax.all_gather(tiles, "panel", axis=1, tiled=True)
    row_count = tile_piece.shape[1]

    def one_slot(slot_index, summed):
        lower_block = lower_blocks[slot_index]
        upper_block = upper_blocks[slot_index]
        tile_part = lax.dynamic_index_in_dim(tile_piece, slot_index, 0, keepdims=False)
        rows_lower = lax.dynamic_slice_in_dim(whole_rows, lower_block * tile_size, row_count, 1)
        rows_upper = lax.dynamic_slice_in_dim(whole_rows, upper_block * tile_size, tile_size, 1)
        direct = (
            jnp.dot(rows_lower, tile_part, preferred_element_type=jnp.float32) * factors[slot_index]
        )
        mirrored = (
            lax.dot_general(
                rows_upper, tile_part, (((1,), (1,)), ((), ())), preferred_element_type=jnp.float32
            )
            * factors[slot_index]
        )
        summed = add_into(summed, direct, upper_block * tile_size)
        summed = add_into(summed, mirrored, lower_block * tile_size)
        return summed

    product = lax.fori_loop(
        0, slot_count, one_slot, jnp.zeros((act_rows, slope_count), jnp.float32)
    )
    owned = lax.psum_scatter(product, "tile", scatter_dimension=1, tiled=True)
    return 2.0 * (owned - c_as.astype(jnp.float32))


def solution(mesh):
    return jax.shard_map(
        body,
        mesh=mesh,
        in_specs=(P("panel", "tile"), P("panel", "tile"), P("tile", "panel", None), P(), P()),
        out_specs=P("panel", "tile"),
        check_vma=False,
    )
```

profile of v0, /device:TPU:1, one launch (start us, length us, event | category | flops | bytes accessed | tf_op | source)
XLA Modules:
  0.0 434.9 jit_solution(17393418335411451259)
XLA Ops:
  6.5 0.0 all-gather.6.cloned.1.call-start
  6.5 0.7 all-gather.6.cloned.1.call-update
  7.3 0.0 all-gather.4.cloned.1.call-start
  7.3 0.7 all-gather.4.cloned.1.call-update
  8.0 0.0 reduce-scatter.4.cloned.1.call-start
  8.1 1.4 fusion.23
  12.1 1.3 fusion.25
  14.0 85.3 %all-gather.6.cloned.1.call-done = bf16[128,240,32]{1,2,0:T(8,128)(2,1)} async-done(((bf16[1,240,32]{1,2,0:T(8,128)(2,1)}), bf16[128,240,32]{1,2,0:T(8,128)(2,1)}) %all-gather.6.cloned.1.call-update) | async-done | bytes 1966096 | tf_op jit(solution)/shard_map/all_gather | solution.py:13
  99.3 2.8 copy.7
  102.1 4.6 %reshape.17 = bf16[30720,32]{0,1:T(8,128)(2,1)} reshape(bf16[128,240,32]{1,0,2:T(8,128)(2,1)S(1)} %copy.7) | data formatting | bytes 3932160
  106.7 79.7 %all-gather.4.cloned.1.call-done = bf16[1,2048,2048]{2,1,0:T(8,128)(2,1)} async-done(((bf16[1,512,2048]{2,1,0:T(8,128)(2,1)}), bf16[1,2048,2048]{2,1,0:T(8,128)(2,1)}) %all-gather.4.cloned.1.call-update) | async-done | bytes 8388624 | tf_op jit(solution)/shard_map/all_gather | solution.py:27
  186.4 0.0 slice-start
  186.4 2.3 broadcast_in_dim.15
  188.7 0.0 slice-start.1
  188.7 6.1 %fusion.7 = f32[32,30720]{1,0:T(8,128)} fusion(f32[32,30720]{1,0:T(8,128)} %broadcast_in_dim.15, s32[]{:T(128)S(6)} %select_n.41, bf16[1,2048,2048]{2,1,0:T(8,128)(2,1)} %all-gather.4.cloned.1.call-done, bf16[30720,32]{0,1:T(8,128)(2,1)} %reshape.17, s32[]{:T(128)S(6)} %select_n.37, f32[]{:T(128)S(6)} %select_n.40), kind=kOutput, calls=%fused_computation.5 | convolution fusion | flops 268500992 | bytes 8781836 | tf_op jit(solution)/shard_map/while/body/eval_jaxpr/dot_general | solution.py:37
  194.8 0.0 slice-done
  194.8 0.0 slice-done.1
  194.8 4.3 fusion.16
  199.1 10.0 %copy.8 = f32[32,30720]{0,1:T(8,128)} copy(f32[32,30720]{1,0:T(8,128)} %fusion.16) | data formatting | bytes 7864320
  209.1 0.0 copy-start
  209.1 0.0 reduce-scatter.4.cloned.1.call-update
  209.1 217.7 %reduce-scatter.4.cloned.1.call-done = f32[240,32]{1,0:T(8,128)} async-done(((f32[30720,32]{1,0:T(8,128)}), f32[240,32]{1,0:T(8,128)}) %reduce-scatter.4.cloned.1.call-update) | async-done | bytes 30736
  426.8 1.0 copy.9
  427.8 0.0 copy-done
  427.8 0.6 subtract_multiply_fusion
  (1 shorter events, 0.0 us)
Async XLA Ops:
  6.5 92.8 %all-gather.6.cloned.1.call-start = ((), (), s32[]{:S(2)}) async-start(), calls=%async_computation.2 | async-start | bytes 2113536 | tf_op jit(solution)/shard_map/all_gather | solution.py:13
  7.3 179.2 %all-gather.4.cloned.1.call-start = ((), (), s32[]{:S(2)}) async-start(), calls=%async_computation.1 | async-start | bytes 10485760 | tf_op jit(solution)/shard_map/all_gather | solution.py:27
  8.0 418.8 %reduce-scatter.4.cloned.1.call-start = ((), (), s32[]{:S(2)}) async-start(), calls=%async_computation.3 | async-start | bytes 15851520
  186.4 8.4 %slice-start = ((s8[8388608]{0:T(1024)(128)(4,1)}), s8[4194304]{0:T(1024)(128)(4,1)S(1)}, s32[]{:S(2)}) async-start(s8[8388608]{0:T(1024)(128)(4,1)} %bitcast.29), calls=%async_computation.4 | async-start | bytes 8388608
  188.7 6.1 %slice-start.1 = ((s8[8388608]{0:T(1024)(128)(4,1)}), s8[4194304]{0:T(1024)(128)(4,1)S(1)}, s32[]{:S(2)}) async-start(s8[8388608]{0:T(1024)(128)(4,1)} %bitcast.29), calls=%async_computation.5 | async-start | bytes 8388608
  209.1 218.7 %copy-start = (bf16[32,240]{1,0:T(8,128)(2,1)S(1)}, bf16[32,240]{1,0:T(8,128)(2,1)}, u32[]{:S(2)}) copy-start(bf16[32,240]{1,0:T(8,128)(2,1)} %param.6) | copy-start | bytes 46084
Sparse Core Ops, SparseCore 0:
  10.5 88.7 all-gather.5
  101.4 84.9 all-gather.3
  209.2 217.5 reduce-scatter.3
where the time goes:
time: 439 us; the launch traced here: 435 us
  waiting for transfers between devices  384 us (87%)
  local copies, waits for them, and re-layouts  20.6 us (5%)
  between operations  16.4 us (4%)
  matrix products  10.4 us (2%)
    unnamed x4, waiting for transfers between devices  219 us
    all_gather x1, waiting for transfers between devices, body(): whole_rows = lax.all_gather(reconstructor, 'tile', axis=1, tiled=True)  85.3 us
    all_gather x1, waiting for transfers between devices, body(): tile_piece = lax.all_gather(tiles, 'panel', axis=1, tiled=True)  79.7 us
    unnamed x9, local copies, waits for them, and re-layouts  15.5 us
  transfers between devices with their start and end apart: 3, of which 3 were waited for; matrix products, arithmetic and copies ran while one was open for 2% of the time, Pallas kernels for 0%

commit v1 on v0

v1 whole, which is shorter than its diff:
```python
import functools

import jax
import jax.numpy as jnp
from jax import lax
from jax.experimental import pallas as pl
from jax.experimental.pallas import tpu as pltpu
from jax.sharding import PartitionSpec as P

MESH = pl.DeviceIdType.MESH
L = 128
F32 = jnp.float32
BF16 = jnp.bfloat16


def wait_for(ref, sem):
    pltpu.make_async_copy(ref, ref, sem).wait()


def kernel(
    cfg,
    pairs_ref, slot_ref, r_ref, x_hbm,
    out_ref,
    xv, img, c_in, own, gath, s3s, afull, aop, bop, dbuf, mbuf, drecv, dsum, mfull, part, acc, q_in, f_own, o_in, tab,
    x_sem, s1s, s1r, s2s, s2r, s3sa, s3ra, s4as, s4ar, s4bs, s4br, ds, dr, ms, mr, ps, pr, qs, qr, os_, or_,
):
    A, W, NX, NZ, NP, NB, T = cfg
    TS = NP * L
    H = TS // NX
    CP = NP * W // L
    G = NX
    GL = TS // G
    GC = NP // G
    t = lax.axis_index("tile")
    p = lax.axis_index("panel")
    z = t // NP
    j = t % NP

    def plane(i):
        return {"tile": z * NP + i}

    def along_z(zz):
        return {"tile": zz * NP + j}

    def along_x(pp):
        return {"panel": pp}

    def send(src, dst, ssem, rsem, dev):
        pltpu.make_async_remote_copy(
            src_ref=src, dst_ref=dst, send_sem=ssem, recv_sem=rsem, device_id=dev, device_id_type=MESH
        ).start()

    x_copy = pltpu.make_async_copy(x_hbm.at[0], xv, x_sem)
    x_copy.start()

    c_in[...] = jnp.zeros_like(c_in)
    o_in[...] = jnp.zeros_like(o_in)
    h0 = (W * j) // L
    off = W * j - L * h0
    row = lax.broadcasted_iota(jnp.int32, (W, 3 * L), 0)
    col = lax.broadcasted_iota(jnp.int32, (W, 3 * L), 1)
    shift = jnp.where(col - row == off, 1.0, 0.0).astype(BF16)
    placed = jnp.dot(r_ref[...], shift, preferred_element_type=F32).astype(BF16)
    for s in range(3):
        img[s] = placed[:, s * L : (s + 1) * L]

    barrier = pltpu.get_barrier_semaphore()

    @pl.loop(1, NP)
    def _(d):
        pl.semaphore_signal(barrier, inc=1, device_id=plane((j + d) % NP), device_id_type=MESH)

    @pl.loop(1, NZ)
    def _(d):
        pl.semaphore_signal(barrier, inc=1, device_id=along_z((z + d) % NZ), device_id_type=MESH)

    @pl.loop(1, NX)
    def _(d):
        pl.semaphore_signal(barrier, inc=1, device_id=along_x((p + d) % NX), device_id_type=MESH)

    pl.semaphore_wait(barrier, NP + NZ + NX - 3)

    for s in range(3):
        h = h0 + s
        live = L * h < W * (j + 1)
        dest = (CP * z + h) % NP
        e = h // NP
        c = jnp.where((off > 0) & (s == 0), 1, 0)

        @pl.when(live & (dest == j))
        def _():
            c_in[e, c] = img[s]

        @pl.when(live & (dest != j))
        def _():
            send(img.at[s], c_in.at[e, c], s1s.at[s], s1r.at[e, c], plane(dest))

    def look(n, got):
        slot = slot_ref[n]
        code = pairs_ref[0, n] * 16 + pairs_ref[1, n]
        return tuple(jnp.where(slot == z * NP + i, code, got[i]) for i in range(NP))

    found = lax.fori_loop(0, T, look, tuple(jnp.int32(-1) for _ in range(NP)))
    mine = jnp.int32(-1)
    for i in range(NP):
        known = jnp.maximum(found[i], 0)
        tab[0, i] = known // 16
        tab[1, i] = known % 16
        mine = jnp.where(j == i, found[i], mine)
    diag = jnp.where(mine // 16 == mine % 16, 0.5, 1.0)
    factor = jnp.where(mine < 0, 0.0, diag).astype(F32)

    hp = (j + (NP - CP % NP) * z) % NP
    for e in range(2):
        h = hp + NP * e
        i_lo = (L * h) // W
        i_hi = (L * h + L - 1) // W

        @pl.when((h < CP) & (i_lo != j))
        def _():
            wait_for(c_in.at[e, 0], s1r.at[e, 0])

        @pl.when((h < CP) & (i_hi != i_lo) & (i_hi != j))
        def _():
            wait_for(c_in.at[e, 1], s1r.at[e, 1])

        mix = (c_in[e, 0].astype(F32) + c_in[e, 1].astype(F32)).astype(BF16)
        own[e] = mix
        gath[2 * z + e] = mix

    @pl.loop(1, NZ)
    def _(d):
        zz = (z + d) % NZ
        send(own, gath.at[pl.ds(2 * z, 2)], s2s.at[d], s2r.at[z], along_z(zz))

    @pl.loop(1, NZ)
    def _(d):
        zz = (z + NZ - d) % NZ
        wait_for(gath.at[pl.ds(2 * zz, 2)], s2r.at[zz])

    p_rows = pl.ds(pl.multiple_of(p * A, A), A)

    def chunk_of(which, i):
        g = tab[which, i] * NP + j
        return gath[2 * (g // CP) + (g % CP) // NP]

    j_lanes = pl.ds(pl.multiple_of(j * L, L), L)
    for which in range(2):

        @pl.loop(1, NP)
        def _(d):
            i = (j + d) % NP
            s3s[which, d] = chunk_of(which, i)
            dst = afull.at[:, j_lanes] if which == 0 else bop.at[p_rows, j_lanes]
            send(s3s.at[which, d], dst, s3sa.at[which, d], s3ra.at[which, j], plane(i))

    afull[:, j_lanes] = chunk_of(0, j)
    bop[p_rows, j_lanes] = chunk_of(1, j)

    @pl.loop(1, NP)
    def _(d):
        i = (j + d) % NP
        wait_for(afull.at[:, pl.ds(pl.multiple_of(i * L, L), L)], s3ra.at[0, i])

    @pl.loop(1, NX)
    def _(d):
        pp = (p + d) % NX
        send(
            afull.at[:, pl.ds(pl.multiple_of(pp * H, H), H)], aop.at[p_rows, :], s4as.at[d], s4ar.at[p], along_x(pp)
        )

    aop[p_rows, :] = afull[:, pl.ds(pl.multiple_of(p * H, H), H)]

    @pl.loop(0, G)
    def _(q):
        @pl.loop(0, GC)
        def _(n):
            i = q * GC + n

            @pl.when(i != j)
            def _():
                wait_for(bop.at[p_rows, pl.ds(pl.multiple_of(i * L, L), L)], s3ra.at[1, i])

        lanes = pl.ds(pl.multiple_of(q * GL, GL), GL)

        @pl.loop(1, NX)
        def _(d):
            pp = (p + d) % NX
            send(bop.at[p_rows, lanes], bop.at[p_rows, lanes], s4bs.at[q, d], s4br.at[q, p], along_x(pp))

    @pl.loop(1, NX)
    def _(d):
        pp = (p + d) % NX
        wait_for(aop.at[pl.ds(pl.multiple_of(pp * A, A), A), :], s4ar.at[pp])

    x_copy.wait()

    @pl.loop(0, G)
    def _(q):
        lanes = pl.ds(pl.multiple_of(q * GL, GL), GL)
        dbuf[q] = jnp.dot(aop[...], xv[:, lanes], preferred_element_type=F32) * factor

        @pl.loop(1, NX)
        def _(d):
            pp = (p + d) % NX
            rows = pl.ds(pl.multiple_of(pp * A, A), A)
            send(dbuf.at[q, rows, :], drecv.at[p, q], ds.at[q, d], dr.at[q, p], along_x(pp))

    mbuf[...] = jnp.zeros_like(mbuf)

    @pl.loop(0, G)
    def _(q):
        lanes = pl.ds(pl.multiple_of(q * GL, GL), GL)

        @pl.loop(1, NX)
        def _(d):
            pp = (p + d) % NX
            wait_for(bop.at[pl.ds(pl.multiple_of(pp * A, A), A), lanes], s4br.at[q, pp])

        mbuf[...] += lax.dot_general(
            bop[:, lanes], xv[:, lanes], (((1,), (1,)), ((), ())), preferred_element_type=F32
        )

    mbuf[...] = mbuf[...] * factor
    p_cols = pl.ds(pl.multiple_of(p * H, H), H)

    @pl.loop(1, NX)
    def _(d):
        pp = (p + d) % NX
        rows = pl.ds(pl.multiple_of(pp * A, A), A)
        send(mbuf.at[rows, :], mfull.at[:, p_cols], ms.at[d], mr.at[p], along_x(pp))

    mfull[:, p_cols] = mbuf[p_rows, :]

    def spread(which, src, i):
        @pl.when(i != j)
        def _():
            send(src, part.at[which, j], ps.at[which, i], pr.at[which, j], plane(i))

        @pl.when(i == j)
        def _():
            part[which, j] = src[...]

    for q in range(G):
        total = dbuf[q, p_rows, :]
        for d in range(1, NX):
            pp = (p + d) % NX
            wait_for(drecv.at[pp, q], dr.at[q, pp])
            total = total + drecv[pp, q]
        for n in range(GC):
            i = q * GC + n
            dsum[i] = total[:, n * L : (n + 1) * L]
            spread(1, dsum.at[i], i)

    @pl.loop(1, NX)
    def _(d):
        pp = (p + d) % NX
        wait_for(mfull.at[:, pl.ds(pl.multiple_of(pp * H, H), H)], mr.at[pp])

    @pl.loop(0, NP)
    def _(i):
        spread(0, mfull.at[:, pl.ds(pl.multiple_of(i * L, L), L)], i)

    @pl.loop(1, NP)
    def _(d):
        i = (j + d) % NP
        wait_for(part.at[1, i], pr.at[1, i])
        wait_for(part.at[0, i], pr.at[0, i])

    acc[NB] = jnp.zeros((A, L), F32)

    @pl.loop(0, NB)
    def _(k):
        total = jnp.zeros((A, L), F32)
        for i in range(NP):
            total = total + jnp.where(tab[0, i] == k, part[0, i], 0.0)
            total = total + jnp.where(tab[1, i] == k, part[1, i], 0.0)
        acc[k] = total

    def first_of(zz):
        return (CP * zz + (j + (NP - CP % NP) * zz) % NP - j) // NP

    @pl.loop(1, NZ)
    def _(d):
        zz = (z + d) % NZ
        send(acc.at[pl.ds(first_of(zz), 2)], q_in.at[z], qs.at[d], qr.at[z], along_z(zz))

    f_own[...] = acc[pl.ds(first_of(z), 2)]

    @pl.loop(1, NZ)
    def _(d):
        zz = (z + NZ - d) % NZ
        wait_for(q_in.at[zz], qr.at[zz])
        f_own[...] += q_in[zz]

    for e in range(2):
        h = hp + NP * e
        i_lo = (L * h) // W
        i_hi = (L * h + L - 1) // W
        for n, i, live in ((0, i_lo, h < CP), (1, i_hi, (h < CP) & (i_hi != i_lo))):
            s = h - (W * i) // L

            @pl.when(live & (i == j))
            def _():
                o_in[s] = f_own[e]

            @pl.when(live & (i != j))
            def _():
                send(f_own.at[e], o_in.at[s], os_.at[e, n], or_.at[s], plane(i))

    for s in range(3):
        h = h0 + s
        holder = (CP * z + h) % NP

        @pl.when((L * h < W * (j + 1)) & (holder != j))
        def _():
            wait_for(o_in.at[s], or_.at[s])

        out_ref[:, s * L : (s + 1) * L] = o_in[s]

    for s in range(3):
        h = h0 + s

        @pl.when((L * h < W * (j + 1)) & ((CP * z + h) % NP != j))
        def _():
            wait_for(img.at[s], s1s.at[s])

    @pl.loop(1, NZ)
    def _(d):
        wait_for(own, s2s.at[d])
        wait_for(acc.at[pl.ds(0, 2)], qs.at[d])

    @pl.loop(1, NP)
    def _(d):
        i = (j + d) % NP
        for which in range(2):
            wait_for(s3s.at[which, d], s3sa.at[which, d])
            wait_for(dsum.at[d], ps.at[which, i])

    @pl.loop(1, NX)
    def _(d):
        wait_for(aop.at[p_rows, :], s4as.at[d])
        wait_for(mbuf.at[p_rows, :], ms.at[d])
        for q in range(G):
            wait_for(bop.at[p_rows, pl.ds(q * GL, GL)], s4bs.at[q, d])
            wait_for(dbuf.at[q, p_rows, :], ds.at[q, d])

    for e in range(2):
        h = hp + NP * e
        i_lo = (L * h) // W
        i_hi = (L * h + L - 1) // W
        for n, i, live in ((0, i_lo, h < CP), (1, i_hi, (h < CP) & (i_hi != i_lo))):

            @pl.when(live & (i != j))
            def _():
                wait_for(f_own.at[e], os_.at[e, n])


def body(n_tile, n_panel, reconstructor, c_as, tiles, tile_pairs, tile_slot):
    A, W = reconstructor.shape
    TS = tiles.shape[2]
    NX = n_panel
    NP = TS // L
    NZ = n_tile // NP
    NB = n_tile * W // TS
    T = tile_slot.shape[0]
    H = TS // NX
    G = NX
    GL = TS // G
    V = pltpu.VMEM
    D = pltpu.SemaphoreType.DMA
    cfg = (A, W, NX, NZ, NP, NB, T)
    chunks = pl.pallas_call(
        functools.partial(kernel, cfg),
        out_shape=jax.ShapeDtypeStruct((A, 3 * L), F32),
        in_specs=[
            pl.BlockSpec(memory_space=pltpu.SMEM),
            pl.BlockSpec(memory_space=pltpu.SMEM),
            pl.BlockSpec(memory_space=pltpu.VMEM),
            pl.BlockSpec(memory_space=pl.ANY),
        ],
        out_specs=pl.BlockSpec(memory_space=pltpu.VMEM),
        scratch_shapes=[
            V((H, TS), BF16),
            V((3, A, L), BF16),
            V((2, 2, A, L), BF16),
            V((2, A, L), BF16),
            V((2 * NZ, A, L), BF16),
            V((2, NP, A, L), BF16),
            V((A, TS), BF16),
            V((A * NX, H), BF16),
            V((A * NX, TS), BF16),
            V((G, A * NX, GL), F32),
            V((A * NX, H), F32),
            V((NX, G, A, GL), F32),
            V((NP, A, L), F32),
            V((A, TS), F32),
            V((2, NP, A, L), F32),
            V((NB + 1, A, L), F32),
            V((NZ, 2, A, L), F32),
            V((2, A, L), F32),
            V((3, A, L), F32),
            pltpu.SMEM((2, NP), jnp.int32),
            D(()),
            D((3,)), D((2, 2)),
            D((NZ,)), D((NZ,)),
            D((2, NP)), D((2, NP)),
            D((NX,)), D((NX,)),
            D((G, NX)), D((G, NX)),
            D((G, NX)), D((G, NX)),
            D((NX,)), D((NX,)),
            D((2, NP)), D((2, NP)),
            D((NZ,)), D((NZ,)),
            D((2, 2)), D((3,)),
        ],
        compiler_params=pltpu.CompilerParams(
            collective_id=0, has_side_effects=True, vmem_limit_bytes=60 * 1024 * 1024
        ),
    )(tile_pairs.T, tile_slot, reconstructor, tiles)
    off = (W * (lax.axis_index("tile") % NP)) % L
    product = lax.dynamic_slice(chunks, (jnp.int32(0), off.astype(jnp.int32)), (A, W))
    return 2.0 * (product - c_as.astype(F32))


def solution(mesh):
    return jax.shard_map(
        functools.partial(body, mesh.shape["tile"], mesh.shape["panel"]),
        mesh=mesh,
        in_specs=(P("panel", "tile"), P("panel", "tile"), P("tile", "panel", None), P(), P()),
        out_specs=P("panel", "tile"),
        check_vma=False,
    )
```

time: 439 us -> 82.2 us (0.19)
  the two profiles are of different devices: /device:TPU:1 before, /device:TPU:24 now
where the time goes in v1:
time: 82.2 us; the launch traced here: 81.9 us
  Pallas kernels  80.4 us (98%)
  other arithmetic  1.5 us (2%)
    pallas_call x1, Pallas kernels, body(): pl.pallas_call(functools.partial(kernel, cfg), out_shape=jax.ShapeDtypeSt...  80.4 us

profile of v1, /device:TPU:24, one launch (start us, length us, event | category | flops | bytes accessed | tf_op | source)
XLA Modules:
  0.0 81.9 jit_solution(14783269563697154217)
XLA Ops:
  0.0 0.0 copy-start
  0.0 80.4 %shard_map.55 = f32[32,384]{1,0:T(8,128)} custom-call(s32[2,120]{1,0:T(2,128)} %bitcast.1, s32[120]{0:T(128)} %slot_ref.1, bf16[32,240]{1,0:T(8,128)(2,1)} %r_ref.1, bf16[1,512,2048]{2,1,0:T(8,128)(2,1)} %x_hbm.1), custom_call_target="tpu_custom_call" | custom-call | tf_op jit(solution)/shard_map/pallas_call | solution.py:373
  80.4 0.0 copy-done
  80.4 1.5 %subtract_multiply_fusion = f32[32,240]{1,0:T(8,128)} fusion(bf16[32,240]{1,0:T(8,128)(2,1)S(1)} %copy-done, f32[32,384]{1,0:T(8,128)} %shard_map.55, s32[]{:T(128)S(6)} %select_n.16), kind=kLoop, calls=%fused_computation | loop fusion | flops 23040 | bytes 76804 | tf_op jit(solution)/shard_map/mul | solution.py:422
Async XLA Ops:
  0.0 80.4 %copy-start = (bf16[32,240]{1,0:T(8,128)(2,1)S(1)}, bf16[32,240]{1,0:T(8,128)(2,1)}, u32[]{:S(2)}) copy-start(bf16[32,240]{1,0:T(8,128)(2,1)} %param.6) | copy-start | bytes 46084

commit v2 on v1

--- a/solution.py
+++ b/solution.py
@@ -11,18 +11,30 @@
 L = 128
 F32 = jnp.float32
 BF16 = jnp.bfloat16
+I16 = jnp.int16
 
 
 def wait_for(ref, sem):
     pltpu.make_async_copy(ref, ref, sem).wait()
+
+
+def code(v):
+    top = jnp.maximum(jnp.max(jnp.abs(v), axis=-2, keepdims=True), 1e-30)
+    return jnp.round(v * (32767.0 / top)).astype(jnp.int32).astype(jnp.int16), top * (1.0 / 32767.0)
+
+
+def value(codes, scale):
+    return codes.astype(jnp.int32).astype(F32) * scale
 
 
 def kernel(
     cfg,
     pairs_ref, slot_ref, r_ref, x_hbm,
     out_ref,
-    xv, img, c_in, own, gath, s3s, afull, aop, bop, dbuf, mbuf, drecv, dsum, mfull, part, acc, q_in, f_own, o_in, tab,
-    x_sem, s1s, s1r, s2s, s2r, s3sa, s3ra, s4as, s4ar, s4bs, s4br, ds, dr, ms, mr, ps, pr, qs, qr, os_, or_,
+    xv, img, c_in, own, gath, s3s, afull, aop, bop, d_own, d_c, d_s, m_c, m_s, d_in, d_in_s, sum_c, sum_s,
+    m_in, m_in_s, part, part_s, part_f, acc, acc_c, acc_s, q_in, q_in_s, f_own, o_in, tab,
+    x_sem, s1s, s1r, s2s, s2r, s3as, s3ar, s3bs, s3br, s4as, s4ar, s4bs, s4br,
+    ds, dr, ms, mr, ps, pr, qs, qr, os_, or_,
 ):
     A, W, NX, NZ, NP, NB, T = cfg
     TS = NP * L
@@ -45,6 +57,10 @@
     def along_x(pp):
         return {"panel": pp}
 
+    def near_first(n):
+        m = NP - 2 - n
+        return NP // 2 + (m + 1) // 2 * (2 * (m % 2) - 1)
+
     def send(src, dst, ssem, rsem, dev):
         pltpu.make_async_remote_copy(
             src_ref=src, dst_ref=dst, send_sem=ssem, recv_sem=rsem, device_id=dev, device_id_type=MESH
@@ -138,144 +154,175 @@
         zz = (z + NZ - d) % NZ
         wait_for(gath.at[pl.ds(2 * zz, 2)], s2r.at[zz])
 
-    p_rows = pl.ds(pl.multiple_of(p * A, A), A)
-
     def chunk_of(which, i):
         g = tab[which, i] * NP + j
         return gath[2 * (g // CP) + (g % CP) // NP]
 
-    j_lanes = pl.ds(pl.multiple_of(j * L, L), L)
-    for which in range(2):
-
-        @pl.loop(1, NP)
-        def _(d):
-            i = (j + d) % NP
-            s3s[which, d] = chunk_of(which, i)
-            dst = afull.at[:, j_lanes] if which == 0 else bop.at[p_rows, j_lanes]
-            send(s3s.at[which, d], dst, s3sa.at[which, d], s3ra.at[which, j], plane(i))
-
-    afull[:, j_lanes] = chunk_of(0, j)
-    bop[p_rows, j_lanes] = chunk_of(1, j)
+    def plane_stage(which, full, ssem, rsem):
+        @pl.loop(0, NP - 1)
+        def _(n):
+            i = (j + near_first(n)) % NP
+            s3s[which, i] = chunk_of(which, i)
+            send(s3s.at[which, i], full(j), ssem.at[i], rsem.at[j], plane(i))
+
+    def b_chunk(i):
+        return bop.at[i, p]
+
+    def a_chunk(i):
+        return afull.at[i]
+
+    plane_stage(1, b_chunk, s3bs, s3br)
+    bop[j, p] = chunk_of(1, j)
+    plane_stage(0, a_chunk, s3as, s3ar)
+    afull[j] = chunk_of(0, j)
+
+    def forward(i):
+        @pl.loop(1, NX)
+        def _(d):
+            send(bop.at[i, p], bop.at[i, p], s4bs.at[i, d], s4br.at[i, p], along_x((p + d) % NX))
+
+    forward(j)
+
+    @pl.loop(0, NP - 1)
+    def _(n):
+        i = (j + NP - near_first(n)) % NP
+        wait_for(bop.at[i, p], s3br.at[i])
+        forward(i)
 
     @pl.loop(1, NP)
     def _(d):
         i = (j + d) % NP
-        wait_for(afull.at[:, pl.ds(pl.multiple_of(i * L, L), L)], s3ra.at[0, i])
+        wait_for(afull.at[i], s3ar.at[i])
 
     @pl.loop(1, NX)
     def _(d):
         pp = (p + d) % NX
-        send(
-            afull.at[:, pl.ds(pl.multiple_of(pp * H, H), H)], aop.at[p_rows, :], s4as.at[d], s4ar.at[p], along_x(pp)
-        )
-
-    aop[p_rows, :] = afull[:, pl.ds(pl.multiple_of(p * H, H), H)]
-
-    @pl.loop(0, G)
-    def _(q):
-        @pl.loop(0, GC)
-        def _(n):
-            i = q * GC + n
-
-            @pl.when(i != j)
-            def _():
-                wait_for(bop.at[p_rows, pl.ds(pl.multiple_of(i * L, L), L)], s3ra.at[1, i])
-
-        lanes = pl.ds(pl.multiple_of(q * GL, GL), GL)
-
-        @pl.loop(1, NX)
-        def _(d):
-            pp = (p + d) % NX
-            send(bop.at[p_rows, lanes], bop.at[p_rows, lanes], s4bs.at[q, d], s4br.at[q, p], along_x(pp))
+        send(afull.at[pl.ds(pp * GC, GC)], aop.at[p], s4as.at[d], s4ar.at[p], along_x(pp))
+
+    aop[p] = afull[pl.ds(p * GC, GC)]
 
     @pl.loop(1, NX)
     def _(d):
         pp = (p + d) % NX
-        wait_for(aop.at[pl.ds(pl.multiple_of(pp * A, A), A), :], s4ar.at[pp])
+        wait_for(aop.at[pp], s4ar.at[pp])
 
     x_copy.wait()
+
+    def side_by_side(pieces):
+        return jnp.concatenate(pieces, axis=1)
+
+    a_rows = jnp.concatenate([side_by_side([aop[pp, n] for n in range(GC)]) for pp in range(NX)], axis=0)
 
     @pl.loop(0, G)
     def _(q):
         lanes = pl.ds(pl.multiple_of(q * GL, GL), GL)
-        dbuf[q] = jnp.dot(aop[...], xv[:, lanes], preferred_element_type=F32) * factor
+        prod = jnp.dot(a_rows, xv[:, lanes], preferred_element_type=F32) * factor
+        for pp in range(NX):
+            for n in range(GC):
+                v = prod[pp * A : (pp + 1) * A, n * L : (n + 1) * L]
+                d_c[q, pp, n], d_s[q, pp, n] = code(v)
+
+                @pl.when(p == pp)
+                def _():
+                    d_own[q, n] = v
 
         @pl.loop(1, NX)
         def _(d):
             pp = (p + d) % NX
-            rows = pl.ds(pl.multiple_of(pp * A, A), A)
-            send(dbuf.at[q, rows, :], drecv.at[p, q], ds.at[q, d], dr.at[q, p], along_x(pp))
-
-    mbuf[...] = jnp.zeros_like(mbuf)
+            send(d_c.at[q, pp], d_in.at[p, q], ds.at[0, q, d], dr.at[0, q, p], along_x(pp))
+            send(d_s.at[q, pp], d_in_s.at[p, q], ds.at[1, q, d], dr.at[1, q, p], along_x(pp))
+
+    prod = jnp.zeros((A * NX, H), F32)
+    for q in range(G):
+
+        @pl.loop(1, NX)
+        def _(d):
+            pp = (p + d) % NX
+
+            @pl.loop(0, GC)
+            def _(n):
+                wait_for(bop.at[q * GC + n, pp], s4br.at[q * GC + n, pp])
+
+        b_cols = side_by_side([bop[q * GC + n].reshape(NX * A, L) for n in range(GC)])
+        prod = prod + lax.dot_general(
+            b_cols, xv[:, q * GL : (q + 1) * GL], (((1,), (1,)), ((), ())), preferred_element_type=F32
+        )
+    prod = prod * factor
+    for pp in range(NX):
+        for n in range(GC):
+            m_c[pp, n], m_s[pp, n] = code(prod[pp * A : (pp + 1) * A, n * L : (n + 1) * L])
+
+    own_chunks = pl.ds(p * GC, GC)
+
+    @pl.loop(1, NX)
+    def _(d):
+        pp = (p + d) % NX
+        send(m_c.at[pp], m_in.at[own_chunks], ms.at[0, d], mr.at[0, p], along_x(pp))
+        send(m_s.at[pp], m_in_s.at[own_chunks], ms.at[1, d], mr.at[1, p], along_x(pp))
+
+    m_in[own_chunks] = m_c[p]
+    m_in_s[own_chunks] = m_s[p]
+
+    def spread(which, codes, scales, i):
+        @pl.when(i != j)
+        def _():
+            send(codes.at[i], part.at[which, j], ps.at[0, which, i], pr.at[0, which, j], plane(i))
+            send(scales.at[i], part_s.at[which, j], ps.at[1, which, i], pr.at[1, which, j], plane(i))
+
+        @pl.when(i == j)
+        def _():
+            part[which, j] = codes[i]
+            part_s[which, j] = scales[i]
 
     @pl.loop(0, G)
     def _(q):
-        lanes = pl.ds(pl.multiple_of(q * GL, GL), GL)
-
         @pl.loop(1, NX)
         def _(d):
             pp = (p + d) % NX
-            wait_for(bop.at[pl.ds(pl.multiple_of(pp * A, A), A), lanes], s4br.at[q, pp])
-
-        mbuf[...] += lax.dot_general(
-            bop[:, lanes], xv[:, lanes], (((1,), (1,)), ((), ())), preferred_element_type=F32
-        )
-
-    mbuf[...] = mbuf[...] * factor
-    p_cols = pl.ds(pl.multiple_of(p * H, H), H)
+            wait_for(d_in.at[pp, q], dr.at[0, q, pp])
+            wait_for(d_in_s.at[pp, q], dr.at[1, q, pp])
+
+        @pl.loop(0, GC)
+        def _(n):
+            total = d_own[q, n]
+            for d in range(1, NX):
+                pp = (p + d) % NX
+                total = total + value(d_in[pp, q, n], d_in_s[pp, q, n])
+            i = q * GC + n
+            sum_c[i], sum_s[i] = code(total)
+            spread(1, sum_c, sum_s, i)
 
     @pl.loop(1, NX)
     def _(d):
         pp = (p + d) % NX
-        rows = pl.ds(pl.multiple_of(pp * A, A), A)
-        send(mbuf.at[rows, :], mfull.at[:, p_cols], ms.at[d], mr.at[p], along_x(pp))
-
-    mfull[:, p_cols] = mbuf[p_rows, :]
-
-    def spread(which, src, i):
-        @pl.when(i != j)
-        def _():
-            send(src, part.at[which, j], ps.at[which, i], pr.at[which, j], plane(i))
-
-        @pl.when(i == j)
-        def _():
-            part[which, j] = src[...]
-
-    for q in range(G):
-        total = dbuf[q, p_rows, :]
-        for d in range(1, NX):
-            pp = (p + d) % NX
-            wait_for(drecv.at[pp, q], dr.at[q, pp])
-            total = total + drecv[pp, q]
-        for n in range(GC):
-            i = q * GC + n
-            dsum[i] = total[:, n * L : (n + 1) * L]
-            spread(1, dsum.at[i], i)
-
-    @pl.loop(1, NX)
-    def _(d):
-        pp = (p + d) % NX
-        wait_for(mfull.at[:, pl.ds(pl.multiple_of(pp * H, H), H)], mr.at[pp])
+        wait_for(m_in.at[pl.ds(pp * GC, GC)], mr.at[0, pp])
+        wait_for(m_in_s.at[pl.ds(pp * GC, GC)], mr.at[1, pp])
 
     @pl.loop(0, NP)
     def _(i):
-        spread(0, mfull.at[:, pl.ds(pl.multiple_of(i * L, L), L)], i)
-
-    @pl.loop(1, NP)
-    def _(d):
-        i = (j + d) % NP
-        wait_for(part.at[1, i], pr.at[1, i])
-        wait_for(part.at[0, i], pr.at[0, i])
+        spread(0, m_in, m_in_s, i)
+
+    for which in (1, 0):
+        part_f[which, j] = value(part[which, j], part_s[which, j])
+
+        @pl.loop(1, NP)
+        def _(d):
+            i = (j + d) % NP
+            wait_for(part.at[which, i], pr.at[0, which, i])
+            wait_for(part_s.at[which, i], pr.at[1, which, i])
+            part_f[which, i] = value(part[which, i], part_s[which, i])
 
     acc[NB] = jnp.zeros((A, L), F32)
+    acc_c[NB], acc_s[NB] = code(acc[NB])
 
     @pl.loop(0, NB)
     def _(k):
         total = jnp.zeros((A, L), F32)
         for i in range(NP):
-            total = total + jnp.where(tab[0, i] == k, part[0, i], 0.0)
-            total = total + jnp.where(tab[1, i] == k, part[1, i], 0.0)
+            total = total + jnp.where(tab[0, i] == k, part_f[0, i], 0.0)
+            total = total + jnp.where(tab[1, i] == k, part_f[1, i], 0.0)
         acc[k] = total
+        acc_c[k], acc_s[k] = code(total)
 
     def first_of(zz):
         return (CP * zz + (j + (NP - CP % NP) * zz) % NP - j) // NP
@@ -283,15 +330,18 @@
     @pl.loop(1, NZ)
     def _(d):
         zz = (z + d) % NZ
-        send(acc.at[pl.ds(first_of(zz), 2)], q_in.at[z], qs.at[d], qr.at[z], along_z(zz))
+        two = pl.ds(first_of(zz), 2)
+        send(acc_c.at[two], q_in.at[z], qs.at[0, d], qr.at[0, z], along_z(zz))
+        send(acc_s.at[two], q_in_s.at[z], qs.at[1, d], qr.at[1, z], along_z(zz))
 
     f_own[...] = acc[pl.ds(first_of(z), 2)]
 
     @pl.loop(1, NZ)
     def _(d):
         zz = (z + NZ - d) % NZ
-        wait_for(q_in.at[zz], qr.at[zz])
-        f_own[...] += q_in[zz]
+        wait_for(q_in.at[zz], qr.at[0, zz])
+        wait_for(q_in_s.at[zz], qr.at[1, zz])
+        f_own[...] += value(q_in[zz], q_in_s[zz])
 
     for e in range(2):
         h = hp + NP * e
@@ -328,22 +378,33 @@
     @pl.loop(1, NZ)
     def _(d):
         wait_for(own, s2s.at[d])
-        wait_for(acc.at[pl.ds(0, 2)], qs.at[d])
-
-    @pl.loop(1, NP)
-    def _(d):
-        i = (j + d) % NP
-        for which in range(2):
-            wait_for(s3s.at[which, d], s3sa.at[which, d])
-            wait_for(dsum.at[d], ps.at[which, i])
-
-    @pl.loop(1, NX)
-    def _(d):
-        wait_for(aop.at[p_rows, :], s4as.at[d])
-        wait_for(mbuf.at[p_rows, :], ms.at[d])
-        for q in range(G):
-            wait_for(bop.at[p_rows, pl.ds(q * GL, GL)], s4bs.at[q, d])
-            wait_for(dbuf.at[q, p_rows, :], ds.at[q, d])
+        wait_for(q_in.at[0], qs.at[0, d])
+        wait_for(q_in_s.at[0], qs.at[1, d])
+
+    @pl.loop(0, NP)
+    def _(i):
+        @pl.when(i != j)
+        def _():
+            wait_for(s3s.at[0, i], s3as.at[i])
+            wait_for(s3s.at[1, i], s3bs.at[i])
+            for which in range(2):
+                wait_for(part.at[which, i], ps.at[0, which, i])
+                wait_for(part_s.at[which, i], ps.at[1, which, i])
+
+        @pl.loop(1, NX)
+        def _(d):
+            wait_for(bop.at[i, p], s4bs.at[i, d])
+
+    @pl.loop(1, NX)
+    def _(d):
+        wait_for(aop.at[p], s4as.at[d])
+        wait_for(m_c.at[p], ms.at[0, d])
+        wait_for(m_s.at[p], ms.at[1, d])
+
+        @pl.loop(0, G)
+        def _(q):
+            wait_for(d_c.at[q, p], ds.at[0, q, d])
+            wait_for(d_s.at[q, p], ds.at[1, q, d])
 
     for e in range(2):
         h = hp + NP * e
@@ -366,7 +427,7 @@
     T = tile_slot.shape[0]
     H = TS // NX
     G = NX
-    GL = TS // G
+    GC = NP // G
     V = pltpu.VMEM
     D = pltpu.SemaphoreType.DMA
     cfg = (A, W, NX, NZ, NP, NB, T)
@@ -387,30 +448,34 @@
             V((2, A, L), BF16),
             V((2 * NZ, A, L), BF16),
             V((2, NP, A, L), BF16),
-            V((A, TS), BF16),
-            V((A * NX, H), BF16),
-            V((A * NX, TS), BF16),
-            V((G, A * NX, GL), F32),
-            V((A * NX, H), F32),
-            V((NX, G, A, GL), F32),
-            V((NP, A, L), F32),
-            V((A, TS), F32),
+            V((NP, A, L), BF16),
+            V((NX, GC, A, L), BF16),
+            V((NP, NX, A, L), BF16),
+            V((G, GC, A, L), F32),
+            V((G, NX, GC, A, L), I16), V((G, NX, GC, 1, L), F32),
+            V((NX, GC, A, L), I16), V((NX, GC, 1, L), F32),
+            V((NX, G, GC, A, L), I16), V((NX, G, GC, 1, L), F32),
+            V((NP, A, L), I16), V((NP, 1, L), F32),
+            V((NP, A, L), I16), V((NP, 1, L), F32),
+            V((2, NP, A, L), I16), V((2, NP, 1, L), F32),
             V((2, NP, A, L), F32),
             V((NB + 1, A, L), F32),
-            V((NZ, 2, A, L), F32),
+            V((NB + 1, A, L), I16), V((NB + 1, 1, L), F32),
+            V((NZ, 2, A, L), I16), V((NZ, 2, 1, L), F32),
             V((2, A, L), F32),
             V((3, A, L), F32),
             pltpu.SMEM((2, NP), jnp.int32),
             D(()),
             D((3,)), D((2, 2)),
             D((NZ,)), D((NZ,)),
-            D((2, NP)), D((2, NP)),
+            D((NP,)), D((NP,)),
+            D((NP,)), D((NP,)),
             D((NX,)), D((NX,)),
-            D((G, NX)), D((G, NX)),
-            D((G, NX)), D((G, NX)),
-            D((NX,)), D((NX,)),
-            D((2, NP)), D((2, NP)),
-            D((NZ,)), D((NZ,)),
+            D((NP, NX)), D((NP, NX)),
+            D((2, G, NX)), D((2, G, NX)),
+            D((2, NX)), D((2, NX)),
+            D((2, 2, NP)), D((2, 2, NP)),
+            D((2, NZ)), D((2, NZ)),
             D((2, 2)), D((3,)),
         ],
         compiler_params=pltpu.CompilerParams(

time: 82.2 us -> 71.6 us (0.87)
  the two profiles are of different devices: /device:TPU:24 before, /device:TPU:1 now
where the time goes in v2:
time: 71.6 us; the launch traced here: 70.3 us
  Pallas kernels  68.8 us (96%)
  other arithmetic  1.5 us (2%)
    pallas_call x1, Pallas kernels, body(): pl.pallas_call(functools.partial(kernel, cfg), out_shape=jax.ShapeDtypeSt...  68.8 us
    mul x1, other arithmetic, body(): return 2.0 * (product - c_as.astype(F32))  1.5 us

profile of v2, /device:TPU:1, one launch (start us, length us, event | category | flops | bytes accessed | tf_op | source)
XLA Modules:
  0.0 70.3 jit_solution(10108361732365291028)
XLA Ops:
  0.0 0.0 copy-start
  0.0 68.8 %shard_map.55 = f32[32,384]{1,0:T(8,128)} custom-call(s32[2,120]{1,0:T(2,128)} %bitcast.1, s32[120]{0:T(128)} %slot_ref.1, bf16[32,240]{1,0:T(8,128)(2,1)} %r_ref.1, bf16[1,512,2048]{2,1,0:T(8,128)(2,1)} %x_hbm.1), custom_call_target="tpu_custom_call" | custom-call | tf_op jit(solution)/shard_map/pallas_call | solution.py:434
  68.8 0.0 copy-done
  68.8 1.5 %subtract_multiply_fusion = f32[32,240]{1,0:T(8,128)} fusion(bf16[32,240]{1,0:T(8,128)(2,1)S(1)} %copy-done, f32[32,384]{1,0:T(8,128)} %shard_map.55, s32[]{:T(128)S(6)} %select_n.16), kind=kLoop, calls=%fused_computation | loop fusion | flops 23040 | bytes 76804 | tf_op jit(solution)/shard_map/mul | solution.py:487
Async XLA Ops:
  0.0 68.8 %copy-start = (bf16[32,240]{1,0:T(8,128)(2,1)S(1)}, bf16[32,240]{1,0:T(8,128)(2,1)}, u32[]{:S(2)}) copy-start(bf16[32,240]{1,0:T(8,128)(2,1)} %param.6) | copy-start | bytes 46084

commit v3 on v2

v3 whole, which is shorter than its diff:
```python
import functools

import jax
import jax.numpy as jnp
from jax import lax
from jax.experimental import pallas as pl
from jax.experimental.pallas import tpu as pltpu
from jax.sharding import PartitionSpec as P

MESH = pl.DeviceIdType.MESH
L = 128
F32 = jnp.float32
BF16 = jnp.bfloat16
I16 = jnp.int16


def wait_for(ref, sem):
    pltpu.make_async_copy(ref, ref, sem).wait()


def div(x, n):
    return lax.div(x, jnp.int32(n))


def rem(x, n):
    return lax.rem(x, jnp.int32(n))


def code(v):
    top = jnp.maximum(jnp.max(jnp.abs(v), axis=-2, keepdims=True), 1e-30)
    return jnp.round(v * (32767.0 / top)).astype(jnp.int32).astype(jnp.int16), top * (1.0 / 32767.0)


def value(codes, scale):
    return codes.astype(jnp.int32).astype(F32) * scale


def kernel(
    cfg,
    pairs_ref, slot_ref, r_ref, x_hbm,
    out_ref,
    xv, img, c_in, own, gath, s3s, afull, a_in_order, aop, bop, d_own, d_c, d_s, m_c, m_s, d_in, d_in_s, sum_c, sum_s,
    m_in, m_in_s, m_out, m_out_s, part, part_s, part_f, acc, acc_c, acc_s, q_in, q_in_s, f_own, o_in, tab, place,
    x_sem, s1s, s1r, s2s, s2r, s3as, s3ar, s3bs, s3br, s4as, s4ar, s4bs, s4br,
    ds, dr, ms, mr, ps, pr, qs, qr, os_, or_,
):
    A, W, NX, NZ, NP, NB, T = cfg
    TS = NP * L
    H = TS // NX
    CP = NP * W // L
    G = NX
    GC = NP // G
    t = lax.axis_index("tile")
    p = lax.axis_index("panel")
    z = t // NP
    j = t % NP

    def plane(i):
        return {"tile": z * NP + i}

    def along_z(zz):
        return {"tile": zz * NP + j}

    def along_x(pp):
        return {"panel": pp}

    def far_first(n):
        return NP // 2 + (n + 1) // 2 * (2 * (n % 2) - 1)

    def near_first(n):
        return far_first(NP - 2 - n)


    def send(src, dst, ssem, rsem, dev):
        pltpu.make_async_remote_copy(
            src_ref=src, dst_ref=dst, send_sem=ssem, recv_sem=rsem, device_id=dev, device_id_type=MESH
        ).start()

    SH = (NP * (W - L) // W) // 2
    BIG = NP * (1 + L * NB // W)

    def chunk_no(k, pos):
        return NP * k + rem(pos + SH + BIG - div(L * NP * k, W), NP)

    def slot_of(k, pos):
        zz = div(chunk_no(k, pos), CP)
        return zz, jnp.where((k > 0) & (chunk_no(k - 1, pos) >= CP * zz), 1, 0)

    def first_of(zz):
        k = div(CP * zz, NP)
        return k + jnp.where(chunk_no(k, j) < CP * zz, 1, 0)

    for i in range(NP):
        pltpu.make_async_copy(x_hbm.at[0, :, pl.ds(i * L, L)], xv.at[i], x_sem).start()

    c_in[...] = jnp.zeros_like(c_in)
    o_in[...] = jnp.zeros_like(o_in)
    barrier = pltpu.get_barrier_semaphore()

    @pl.loop(1, NP)
    def _(d):
        pl.semaphore_signal(barrier, inc=1, device_id=plane((j + d) % NP), device_id_type=MESH)

    @pl.loop(1, NZ)
    def _(d):
        pl.semaphore_signal(barrier, inc=1, device_id=along_z((z + d) % NZ), device_id_type=MESH)

    @pl.loop(1, NX)
    def _(d):
        pl.semaphore_signal(barrier, inc=1, device_id=along_x((p + d) % NX), device_id_type=MESH)

    h0 = (W * j) // L
    off = W * j - L * h0
    row = lax.broadcasted_iota(jnp.int32, (W, 3 * L), 0)
    col = lax.broadcasted_iota(jnp.int32, (W, 3 * L), 1)
    shift = jnp.where(col - row == off, 1.0, 0.0).astype(BF16)
    placed = jnp.dot(r_ref[...], shift, preferred_element_type=F32).astype(BF16)
    for s in range(3):
        img[s] = placed[:, s * L : (s + 1) * L]

    pl.semaphore_wait(barrier, NP + NZ + NX - 3)

    for s in range(3):
        h = h0 + s
        live = L * h < W * (j + 1)
        block, rest = div(CP * z + h, NP), rem(CP * z + h, NP)
        dest = rem(rest + div(L * NP * block, W) + NP - SH, NP)
        _, e = slot_of(block, dest)
        c = jnp.where((off > 0) & (s == 0), 1, 0)

        @pl.when(live & (dest == j))
        def _():
            c_in[e, c] = img[s]

        @pl.when(live & (dest != j))
        def _():
            send(img.at[s], c_in.at[e, c], s1s.at[s], s1r.at[e, c], plane(dest))

    def look(n, got):
        slot = slot_ref[n]
        code = pairs_ref[0, n] * 16 + pairs_ref[1, n]
        return tuple(jnp.where(slot == z * NP + i, code, got[i]) for i in range(NP))

    found = lax.fori_loop(0, T, look, tuple(jnp.int32(-1) for _ in range(NP)))
    mine = jnp.int32(-1)
    for i in range(NP):
        known = jnp.maximum(found[i], 0)
        for which, block in enumerate((known // 16, known % 16)):
            tab[which, i] = block
            zz, e = slot_of(block, j)
            place[which, i] = 2 * zz + e
        mine = jnp.where(j == i, found[i], mine)
    known = jnp.maximum(mine, 0)
    turn_a = rem(div(L * NP * (known // 16), W) + NP - SH, NP)
    turn_b = rem(div(L * NP * (known % 16), W) + NP - SH, NP)
    diag = jnp.where(mine // 16 == mine % 16, 0.5, 1.0)
    factor = jnp.where(mine < 0, 0.0, diag).astype(F32)

    mine_first = first_of(z)

    def chunk_at(e):
        h = chunk_no(mine_first + e, j) - CP * z
        return h, (mine_first + e < NB) & (h < CP)

    for e in range(2):
        h, live = chunk_at(e)
        i_lo = (L * h) // W
        i_hi = (L * h + L - 1) // W

        @pl.when(live & (i_lo != j))
        def _():
            wait_for(c_in.at[e, 0], s1r.at[e, 0])

        @pl.when(live & (i_hi != i_lo) & (i_hi != j))
        def _():
            wait_for(c_in.at[e, 1], s1r.at[e, 1])

        mix = (c_in[e, 0].astype(F32) + c_in[e, 1].astype(F32)).astype(BF16)
        own[e] = mix
        gath[2 * z + e] = mix

    @pl.loop(1, NZ)
    def _(n):
        d = NZ // 2 + n // 2 * (2 * ((n - 1) % 2) - 1)
        zz = (z + d) % NZ
        send(own, gath.at[pl.ds(2 * z, 2)], s2s.at[d], s2r.at[z], along_z(zz))

    @pl.loop(1, NZ)
    def _(d):
        zz = (z + NZ - d) % NZ
        wait_for(gath.at[pl.ds(2 * zz, 2)], s2r.at[zz])

    def chunk_of(which, i):
        return gath[place[which, i]]

    def plane_stage(which, full, ssem, rsem):
        @pl.loop(0, NP - 1)
        def _(n):
            i = (j + near_first(n)) % NP
            s3s[which, i] = chunk_of(which, i)
            send(s3s.at[which, i], full(j), ssem.at[i], rsem.at[j], plane(i))

    def b_chunk(i):
        return bop.at[i, p]

    def a_chunk(i):
        return afull.at[i]

    plane_stage(1, b_chunk, s3bs, s3br)
    bop[j, p] = chunk_of(1, j)
    plane_stage(0, a_chunk, s3as, s3ar)
    afull[j] = chunk_of(0, j)

    def forward(i):
        @pl.loop(1, NX)
        def _(d):
            send(bop.at[i, p], bop.at[i, p], s4bs.at[i, d], s4br.at[i, p], along_x((p + d) % NX))

    forward(j)

    @pl.loop(0, NP - 1)
    def _(n):
        i = (j + NP - near_first(n)) % NP
        wait_for(bop.at[i, p], s3br.at[i])
        forward(i)

    wait_for(xv, x_sem)

    def x_chunk(i):
        return xv[rem(i + NP - turn_b, NP)]

    def side_by_side(pieces):
        return jnp.concatenate(pieces, axis=1)

    @pl.loop(1, NP)
    def _(d):
        i = (j + d) % NP
        wait_for(afull.at[i], s3ar.at[i])

    for i in range(NP):
        a_in_order[i] = afull[rem(i + turn_a, NP)]

    @pl.loop(1, NX)
    def _(d):
        pp = (p + d) % NX
        send(a_in_order.at[pl.ds(pp * GC, GC)], aop.at[p], s4as.at[d], s4ar.at[p], along_x(pp))

    aop[p] = a_in_order[pl.ds(p * GC, GC)]

    prod = jnp.zeros((A * NX, H), F32)
    for q in range(G):

        @pl.loop(1, NX)
        def _(d):
            pp = (p + d) % NX

            @pl.loop(0, GC)
            def _(n):
                wait_for(bop.at[q * GC + n, pp], s4br.at[q * GC + n, pp])

        b_cols = side_by_side([bop[q * GC + n].reshape(NX * A, L) for n in range(GC)])
        x_cols = side_by_side([x_chunk(q * GC + n) for n in range(GC)])
        prod = prod + lax.dot_general(b_cols, x_cols, (((1,), (1,)), ((), ())), preferred_element_type=F32)
    prod = prod * factor
    for pp in range(NX):
        for n in range(GC):
            m_c[pp, n], m_s[pp, n] = code(prod[pp * A : (pp + 1) * A, n * L : (n + 1) * L])

    own_chunks = pl.ds(p * GC, GC)

    @pl.loop(1, NX)
    def _(d):
        pp = (p + d) % NX
        send(m_c.at[pp], m_in.at[own_chunks], ms.at[0, d], mr.at[0, p], along_x(pp))
        send(m_s.at[pp], m_in_s.at[own_chunks], ms.at[1, d], mr.at[1, p], along_x(pp))

    m_in[own_chunks] = m_c[p]
    m_in_s[own_chunks] = m_s[p]

    @pl.loop(1, NX)
    def _(d):
        pp = (p + d) % NX
        wait_for(aop.at[pp], s4ar.at[pp])

    a_rows = jnp.concatenate([side_by_side([aop[pp, n] for n in range(GC)]) for pp in range(NX)], axis=0)

    def group(n):
        return (n + j // GC) % G

    @pl.loop(0, G)
    def _(step):
        q = group(step)
        x_cols = side_by_side([x_chunk(q * GC + n) for n in range(GC)])
        prod = jnp.dot(a_rows, x_cols, preferred_element_type=F32) * factor
        for pp in range(NX):
            for n in range(GC):
                v = prod[pp * A : (pp + 1) * A, n * L : (n + 1) * L]
                d_c[q, pp, n], d_s[q, pp, n] = code(v)

                @pl.when(p == pp)
                def _():
                    d_own[q, n] = v

        @pl.loop(1, NX)
        def _(d):
            pp = (p + d) % NX
            send(d_c.at[q, pp], d_in.at[p, q], ds.at[0, q, d], dr.at[0, q, p], along_x(pp))
            send(d_s.at[q, pp], d_in_s.at[p, q], ds.at[1, q, d], dr.at[1, q, p], along_x(pp))

    def spread(which, codes, scales, i):
        @pl.when(i != j)
        def _():
            send(codes.at[i], part.at[which, j], ps.at[0, which, i], pr.at[0, which, j], plane(i))
            send(scales.at[i], part_s.at[which, j], ps.at[1, which, i], pr.at[1, which, j], plane(i))

        @pl.when(i == j)
        def _():
            part[which, j] = codes[i]
            part_s[which, j] = scales[i]

    @pl.loop(1, NX)
    def _(d):
        pp = (p + d) % NX
        wait_for(m_in.at[pl.ds(pp * GC, GC)], mr.at[0, pp])
        wait_for(m_in_s.at[pl.ds(pp * GC, GC)], mr.at[1, pp])

    @pl.loop(0, NP)
    def _(n):
        i = (j + far_first(n)) % NP
        r = rem(i + NP - turn_a, NP)
        m_out[i] = m_in[r]
        m_out_s[i] = m_in_s[r]
        spread(0, m_out, m_out_s, i)

    @pl.loop(0, G)
    def _(step):
        q = group(step)

        @pl.loop(1, NX)
        def _(d):
            pp = (p + d) % NX
            wait_for(d_in.at[pp, q], dr.at[0, q, pp])
            wait_for(d_in_s.at[pp, q], dr.at[1, q, pp])

        @pl.loop(0, GC)
        def _(turn):
            n = (turn + j) % GC
            total = d_own[q, n]
            for d in range(1, NX):
                pp = (p + d) % NX
                total = total + value(d_in[pp, q, n], d_in_s[pp, q, n])
            i = q * GC + n
            sum_c[i], sum_s[i] = code(total)
            spread(1, sum_c, sum_s, i)

    for which in (0, 1):

        @pl.loop(1, NP)
        def _(d):
            i = (j + d) % NP
            wait_for(part.at[which, i], pr.at[0, which, i])
            wait_for(part_s.at[which, i], pr.at[1, which, i])

        for i in range(NP):
            part_f[i] = value(part[which, i], part_s[which, i])

        @pl.loop(0, NB)
        def _(k):
            total = acc[k] if which else jnp.zeros((A, L), F32)
            for i in range(NP):
                total = total + jnp.where(tab[which, i] == k, part_f[i], 0.0)
            acc[k] = total
            if which:
                acc_c[k], acc_s[k] = code(total)

    acc_c[NB], acc_s[NB] = code(jnp.zeros((A, L), F32))

    @pl.loop(1, NZ)
    def _(n):
        d = NZ // 2 + n // 2 * (2 * ((n - 1) % 2) - 1)
        zz = (z + d) % NZ
        two = pl.ds(first_of(zz), 2)
        send(acc_c.at[two], q_in.at[z], qs.at[0, d], qr.at[0, z], along_z(zz))
        send(acc_s.at[two], q_in_s.at[z], qs.at[1, d], qr.at[1, z], along_z(zz))

    f_own[0] = acc[mine_first]
    f_own[1] = acc[jnp.minimum(mine_first + 1, NB - 1)]

    @pl.loop(1, NZ)
    def _(d):
        zz = (z + NZ - d) % NZ
        wait_for(q_in.at[zz], qr.at[0, zz])
        wait_for(q_in_s.at[zz], qr.at[1, zz])
        f_own[...] += value(q_in[zz], q_in_s[zz])

    for e in range(2):
        h, here = chunk_at(e)
        i_lo = (L * h) // W
        i_hi = (L * h + L - 1) // W
        for n, i, live in ((0, i_lo, here), (1, i_hi, here & (i_hi != i_lo))):
            s = h - (W * i) // L

            @pl.when(live & (i == j))
            def _():
                o_in[s] = f_own[e]

            @pl.when(live & (i != j))
            def _():
                send(f_own.at[e], o_in.at[s], os_.at[e, n], or_.at[s], plane(i))

    for s in range(3):
        h = h0 + s
        block, rest = div(CP * z + h, NP), rem(CP * z + h, NP)
        holder = rem(rest + div(L * NP * block, W) + NP - SH, NP)

        @pl.when((L * h < W * (j + 1)) & (holder != j))
        def _():
            wait_for(o_in.at[s], or_.at[s])

    wide = side_by_side([o_in[s] for s in range(3)])
    out_ref[...] = pltpu.roll(wide, rem(3 * L - off, 3 * L), 1)[:, :W]

    for s in range(3):
        h = h0 + s

        block, rest = div(CP * z + h, NP), rem(CP * z + h, NP)
        holder = rem(rest + div(L * NP * block, W) + NP - SH, NP)

        @pl.when((L * h < W * (j + 1)) & (holder != j))
        def _():
            wait_for(img.at[s], s1s.at[s])

    @pl.loop(1, NZ)
    def _(d):
        wait_for(own, s2s.at[d])
        wait_for(q_in.at[0], qs.at[0, d])
        wait_for(q_in_s.at[0], qs.at[1, d])

    @pl.loop(0, NP)
    def _(i):
        @pl.when(i != j)
        def _():
            wait_for(s3s.at[0, i], s3as.at[i])
            wait_for(s3s.at[1, i], s3bs.at[i])
            for which in range(2):
                wait_for(part.at[which, i], ps.at[0, which, i])
                wait_for(part_s.at[which, i], ps.at[1, which, i])

        @pl.loop(1, NX)
        def _(d):
            wait_for(bop.at[i, p], s4bs.at[i, d])

    @pl.loop(1, NX)
    def _(d):
        wait_for(aop.at[p], s4as.at[d])
        wait_for(m_c.at[p], ms.at[0, d])
        wait_for(m_s.at[p], ms.at[1, d])

        @pl.loop(0, G)
        def _(q):
            wait_for(d_c.at[q, p], ds.at[0, q, d])
            wait_for(d_s.at[q, p], ds.at[1, q, d])

    for e in range(2):
        h, here = chunk_at(e)
        i_lo = (L * h) // W
        i_hi = (L * h + L - 1) // W
        for n, i, live in ((0, i_lo, here), (1, i_hi, here & (i_hi != i_lo))):

            @pl.when(live & (i != j))
            def _():
                wait_for(f_own.at[e], os_.at[e, n])


def body(n_tile, n_panel, reconstructor, c_as, tiles, tile_pairs, tile_slot):
    A, W = reconstructor.shape
    TS = tiles.shape[2]
    NX = n_panel
    NP = TS // L
    NZ = n_tile // NP
    NB = n_tile * W // TS
    T = tile_slot.shape[0]
    H = TS // NX
    G = NX
    GC = NP // G
    V = pltpu.VMEM
    D = pltpu.SemaphoreType.DMA
    cfg = (A, W, NX, NZ, NP, NB, T)
    product = pl.pallas_call(
        functools.partial(kernel, cfg),
        out_shape=jax.ShapeDtypeStruct((A, W), F32),
        in_specs=[
            pl.BlockSpec(memory_space=pltpu.SMEM),
            pl.BlockSpec(memory_space=pltpu.SMEM),
            pl.BlockSpec(memory_space=pltpu.VMEM),
            pl.BlockSpec(memory_space=pl.ANY),
        ],
        out_specs=pl.BlockSpec(memory_space=pltpu.VMEM),
        scratch_shapes=[
            V((NP, H, L), BF16),
            V((3, A, L), BF16),
            V((2, 2, A, L), BF16),
            V((2, A, L), BF16),
            V((2 * NZ, A, L), BF16),
            V((2, NP, A, L), BF16),
            V((NP, A, L), BF16), V((NP, A, L), BF16),
            V((NX, GC, A, L), BF16),
            V((NP, NX, A, L), BF16),
            V((G, GC, A, L), F32),
            V((G, NX, GC, A, L), I16), V((G, NX, GC, 1, L), F32),
            V((NX, GC, A, L), I16), V((NX, GC, 1, L), F32),
            V((NX, G, GC, A, L), I16), V((NX, G, GC, 1, L), F32),
            V((NP, A, L), I16), V((NP, 1, L), F32),
            V((NP, A, L), I16), V((NP, 1, L), F32),
            V((NP, A, L), I16), V((NP, 1, L), F32),
            V((2, NP, A, L), I16), V((2, NP, 1, L), F32),
            V((NP, A, L), F32),
            V((NB, A, L), F32),
            V((NB + 1, A, L), I16), V((NB + 1, 1, L), F32),
            V((NZ, 2, A, L), I16), V((NZ, 2, 1, L), F32),
            V((2, A, L), F32),
            V((3, A, L), F32),
            pltpu.SMEM((2, NP), jnp.int32), pltpu.SMEM((2, NP), jnp.int32),
            D(()),
            D((3,)), D((2, 2)),
            D((NZ,)), D((NZ,)),
            D((NP,)), D((NP,)),
            D((NP,)), D((NP,)),
            D((NX,)), D((NX,)),
            D((NP, NX)), D((NP, NX)),
            D((2, G, NX)), D((2, G, NX)),
            D((2, NX)), D((2, NX)),
            D((2, 2, NP)), D((2, 2, NP)),
            D((2, NZ)), D((2, NZ)),
            D((2, 2)), D((3,)),
        ],
        compiler_params=pltpu.CompilerParams(
            collective_id=0, has_side_effects=True, vmem_limit_bytes=60 * 1024 * 1024
        ),
    )(tile_pairs.T, tile_slot, reconstructor, tiles)
    return 2.0 * (product - c_as.astype(F32))


def solution(mesh):
    return jax.shard_map(
        functools.partial(body, mesh.shape["tile"], mesh.shape["panel"]),
        mesh=mesh,
        in_specs=(P("panel", "tile"), P("panel", "tile"), P("tile", "panel", None), P(), P()),
        out_specs=P("panel", "tile"),
        check_vma=False,
    )
```

time: 71.6 us -> 67.8 us (0.947); the launches traced: 70.3 us -> 67.5 us
  Pallas kernels: 68.8 us -> 66.1 us
    pallas_call x1, Pallas kernels: 68.8 us -> 66.1 us  [body(): pl.pallas_call(functools.partial(kernel, cfg), out_shape=jax.ShapeDtypeSt...]
where the time goes in v3:
time: 67.8 us; the launch traced here: 67.5 us
  Pallas kernels  66.1 us (97%)
  other arithmetic  1.38 us (2%)
    pallas_call x1, Pallas kernels, body(): pl.pallas_call(functools.partial(kernel, cfg), out_shape=jax.ShapeDtypeSt...  66.1 us
    mul x1, other arithmetic, body(): return 2.0 * (product - c_as.astype(F32))  1.38 us

profile of v3, /device:TPU:1, one launch (start us, length us, event | category | flops | bytes accessed | tf_op | source)
XLA Modules:
  0.0 67.5 jit_solution(7835828332875560315)
XLA Ops:
  0.0 0.0 copy-start
  0.0 66.1 %shard_map.55 = f32[32,240]{1,0:T(8,128)} custom-call(s32[2,120]{1,0:T(2,128)} %bitcast.1, s32[120]{0:T(128)} %slot_ref.1, bf16[32,240]{1,0:T(8,128)(2,1)} %r_ref.1, bf16[1,512,2048]{2,1,0:T(8,128)(2,1)} %x_hbm.1), custom_call_target="tpu_custom_call" | custom-call | tf_op jit(solution)/shard_map/pallas_call | solution.py:489
  66.1 0.0 copy-done
  66.1 1.4 %subtract_multiply_fusion = f32[32,240]{1,0:T(8,128)} fusion(f32[32,240]{1,0:T(8,128)} %shard_map.55, bf16[32,240]{1,0:T(8,128)(2,1)S(1)} %copy-done), kind=kLoop, calls=%fused_computation | loop fusion | flops 23040 | bytes 76800 | tf_op jit(solution)/shard_map/mul | solution.py:541
Async XLA Ops:
  0.0 66.1 %copy-start = (bf16[32,240]{1,0:T(8,128)(2,1)S(1)}, bf16[32,240]{1,0:T(8,128)(2,1)}, u32[]{:S(2)}) copy-start(bf16[32,240]{1,0:T(8,128)(2,1)} %param.6) | copy-start | bytes 46084

commit v4 on v3

--- a/solution.py
+++ b/solution.py
@@ -39,9 +39,9 @@
     cfg,
     pairs_ref, slot_ref, r_ref, x_hbm,
     out_ref,
-    xv, img, c_in, own, gath, s3s, afull, a_in_order, aop, bop, d_own, d_c, d_s, m_c, m_s, d_in, d_in_s, sum_c, sum_s,
+    xv, wide, img, c_in, own, gath, s3s, afull, a_in_order, aop, bop, d_own, d_c, d_s, m_c, m_s, d_in, d_in_s, sum_c, sum_s,
     m_in, m_in_s, m_out, m_out_s, part, part_s, part_f, acc, acc_c, acc_s, q_in, q_in_s, f_own, o_in, tab, place,
-    x_sem, s1s, s1r, s2s, s2r, s3as, s3ar, s3bs, s3br, s4as, s4ar, s4bs, s4br,
+    x_sem, passed_z, passed_plane, s1s, s1r, s2s, s2r, s3as, s3ar, s3bs, s3br, s4as, s4ar, s4bs, s4br,
     ds, dr, ms, mr, ps, pr, qs, qr, os_, or_,
 ):
     A, W, NX, NZ, NP, NB, T = cfg
@@ -90,20 +90,32 @@
         k = div(CP * zz, NP)
         return k + jnp.where(chunk_no(k, j) < CP * zz, 1, 0)
 
-    for i in range(NP):
-        pltpu.make_async_copy(x_hbm.at[0, :, pl.ds(i * L, L)], xv.at[i], x_sem).start()
 
     c_in[...] = jnp.zeros_like(c_in)
     o_in[...] = jnp.zeros_like(o_in)
     barrier = pltpu.get_barrier_semaphore()
 
-    @pl.loop(1, NP)
-    def _(d):
-        pl.semaphore_signal(barrier, inc=1, device_id=plane((j + d) % NP), device_id_type=MESH)
-
-    @pl.loop(1, NZ)
-    def _(d):
-        pl.semaphore_signal(barrier, inc=1, device_id=along_z((z + d) % NZ), device_id_type=MESH)
+    REACH = 2
+    CHIPS = NP // 2
+    near_plane = 2 * min(CHIPS, 2 * REACH + 1) - 1
+    near_z = min(NZ, 2 * REACH + 1) - 1
+
+    def tell_plane(sem):
+        for away in range(-min(REACH, (CHIPS - 1) // 2), min(REACH, CHIPS // 2) + 1):
+            for core in range(2):
+                i = 2 * ((j // 2 + away + CHIPS) % CHIPS) + core
+
+                @pl.when(i != j)
+                def _():
+                    pl.semaphore_signal(sem, inc=1, device_id=plane(i), device_id_type=MESH)
+
+    def tell_z(sem):
+        for d in range(1, NZ):
+            if min(d, NZ - d) <= REACH:
+                pl.semaphore_signal(sem, inc=1, device_id=along_z((z + d) % NZ), device_id_type=MESH)
+
+    tell_plane(barrier)
+    tell_z(barrier)
 
     @pl.loop(1, NX)
     def _(d):
@@ -111,14 +123,13 @@
 
     h0 = (W * j) // L
     off = W * j - L * h0
-    row = lax.broadcasted_iota(jnp.int32, (W, 3 * L), 0)
-    col = lax.broadcasted_iota(jnp.int32, (W, 3 * L), 1)
-    shift = jnp.where(col - row == off, 1.0, 0.0).astype(BF16)
-    placed = jnp.dot(r_ref[...], shift, preferred_element_type=F32).astype(BF16)
+    wide[...] = jnp.zeros_like(wide)
+    wide[:, :W] = r_ref[...].astype(F32)
+    placed = pltpu.roll(wide[...], off, 1).astype(BF16)
     for s in range(3):
         img[s] = placed[:, s * L : (s + 1) * L]
 
-    pl.semaphore_wait(barrier, NP + NZ + NX - 3)
+    pl.semaphore_wait(barrier, near_plane + near_z + NX - 1)
 
     for s in range(3):
         h = h0 + s
@@ -135,6 +146,42 @@
         @pl.when(live & (dest != j))
         def _():
             send(img.at[s], c_in.at[e, c], s1s.at[s], s1r.at[e, c], plane(dest))
+
+    tell_z(passed_z)
+    tell_plane(passed_plane)
+
+    for i in range(NP):
+        pltpu.make_async_copy(x_hbm.at[0, :, pl.ds(i * L, L)], xv.at[i], x_sem).start()
+
+    mine_first = first_of(z)
+
+    def chunk_at(e):
+        h = chunk_no(mine_first + e, j) - CP * z
+        return h, (mine_first + e < NB) & (h < CP)
+
+    for e in range(2):
+        h, live = chunk_at(e)
+        i_lo = (L * h) // W
+        i_hi = (L * h + L - 1) // W
+
+        @pl.when(live & (i_lo != j))
+        def _():
+            wait_for(c_in.at[e, 0], s1r.at[e, 0])
+
+        @pl.when(live & (i_hi != i_lo) & (i_hi != j))
+        def _():
+            wait_for(c_in.at[e, 1], s1r.at[e, 1])
+
+        mix = (c_in[e, 0].astype(F32) + c_in[e, 1].astype(F32)).astype(BF16)
+        own[e] = mix
+        gath[2 * z + e] = mix
+
+    pl.semaphore_wait(passed_z, near_z)
+    @pl.loop(1, NZ)
+    def _(n):
+        d = NZ // 2 + n // 2 * (2 * ((n - 1) % 2) - 1)
+        zz = (z + d) % NZ
+        send(own, gath.at[pl.ds(2 * z, 2)], s2s.at[d], s2r.at[z], along_z(zz))
 
     def look(n, got):
         slot = slot_ref[n]
@@ -156,35 +203,6 @@
     diag = jnp.where(mine // 16 == mine % 16, 0.5, 1.0)
     factor = jnp.where(mine < 0, 0.0, diag).astype(F32)
 
-    mine_first = first_of(z)
-
-    def chunk_at(e):
-        h = chunk_no(mine_first + e, j) - CP * z
-        return h, (mine_first + e < NB) & (h < CP)
-
-    for e in range(2):
-        h, live = chunk_at(e)
-        i_lo = (L * h) // W
-        i_hi = (L * h + L - 1) // W
-
-        @pl.when(live & (i_lo != j))
-        def _():
-            wait_for(c_in.at[e, 0], s1r.at[e, 0])
-
-        @pl.when(live & (i_hi != i_lo) & (i_hi != j))
-        def _():
-            wait_for(c_in.at[e, 1], s1r.at[e, 1])
-
-        mix = (c_in[e, 0].astype(F32) + c_in[e, 1].astype(F32)).astype(BF16)
-        own[e] = mix
-        gath[2 * z + e] = mix
-
-    @pl.loop(1, NZ)
-    def _(n):
-        d = NZ // 2 + n // 2 * (2 * ((n - 1) % 2) - 1)
-        zz = (z + d) % NZ
-        send(own, gath.at[pl.ds(2 * z, 2)], s2s.at[d], s2r.at[z], along_z(zz))
-
     @pl.loop(1, NZ)
     def _(d):
         zz = (z + NZ - d) % NZ
@@ -192,6 +210,8 @@
 
     def chunk_of(which, i):
         return gath[place[which, i]]
+
+    pl.semaphore_wait(passed_plane, near_plane)
 
     def plane_stage(which, full, ssem, rsem):
         @pl.loop(0, NP - 1)
@@ -417,8 +437,8 @@
         def _():
             wait_for(o_in.at[s], or_.at[s])
 
-    wide = side_by_side([o_in[s] for s in range(3)])
-    out_ref[...] = pltpu.roll(wide, rem(3 * L - off, 3 * L), 1)[:, :W]
+    shifted = side_by_side([o_in[s] for s in range(3)])
+    out_ref[...] = pltpu.roll(shifted, rem(3 * L - off, 3 * L), 1)[:, :W]
 
     for s in range(3):
         h = h0 + s
@@ -498,6 +518,7 @@
         out_specs=pl.BlockSpec(memory_space=pltpu.VMEM),
         scratch_shapes=[
             V((NP, H, L), BF16),
+            V((A, 3 * L), F32),
             V((3, A, L), BF16),
             V((2, 2, A, L), BF16),
             V((2, A, L), BF16),
@@ -522,6 +543,7 @@
             V((3, A, L), F32),
             pltpu.SMEM((2, NP), jnp.int32), pltpu.SMEM((2, NP), jnp.int32),
             D(()),
+            pltpu.SemaphoreType.REGULAR, pltpu.SemaphoreType.REGULAR,
             D((3,)), D((2, 2)),
             D((NZ,)), D((NZ,)),
             D((NP,)), D((NP,)),

time: 67.8 us -> 66.7 us (0.984)
  Pallas kernels: 66.1 us -> 65.1 us
    pallas_call x1, Pallas kernels: 66.1 us -> 65.1 us  [body(): pl.pallas_call(functools.partial(kernel, cfg), out_shape=jax.ShapeDtypeSt...]
where the time goes in v4:
time: 66.7 us; the launch traced here: 66.5 us
  Pallas kernels  65.1 us (98%)
  other arithmetic  1.38 us (2%)
    pallas_call x1, Pallas kernels, body(): pl.pallas_call(functools.partial(kernel, cfg), out_shape=jax.ShapeDtypeSt...  65.1 us
    mul x1, other arithmetic, body(): return 2.0 * (product - c_as.astype(F32))  1.38 us

profile of v4, /device:TPU:1, one launch (start us, length us, event | category | flops | bytes accessed | tf_op | source)
XLA Modules:
  0.0 66.5 jit_solution(18275916228355102345)
XLA Ops:
  0.0 0.0 copy-start
  0.0 65.1 %shard_map.55 = f32[32,240]{1,0:T(8,128)} custom-call(s32[2,120]{1,0:T(2,128)} %bitcast.1, s32[120]{0:T(128)} %slot_ref.1, bf16[32,240]{1,0:T(8,128)(2,1)} %r_ref.1, bf16[1,512,2048]{2,1,0:T(8,128)(2,1)} %x_hbm.1), custom_call_target="tpu_custom_call" | custom-call | tf_op jit(solution)/shard_map/pallas_call | solution.py:509
  65.1 0.0 copy-done
  65.1 1.4 %subtract_multiply_fusion = f32[32,240]{1,0:T(8,128)} fusion(f32[32,240]{1,0:T(8,128)} %shard_map.55, bf16[32,240]{1,0:T(8,128)(2,1)S(1)} %copy-done), kind=kLoop, calls=%fused_computation | loop fusion | flops 23040 | bytes 76800 | tf_op jit(solution)/shard_map/mul | solution.py:563
Async XLA Ops:
  0.0 65.1 %copy-start = (bf16[32,240]{1,0:T(8,128)(2,1)S(1)}, bf16[32,240]{1,0:T(8,128)(2,1)}, u32[]{:S(2)}) copy-start(bf16[32,240]{1,0:T(8,128)(2,1)} %param.6) | copy-start | bytes 46084

commit v5 on v4

--- a/solution.py
+++ b/solution.py
@@ -231,18 +231,26 @@
     plane_stage(0, a_chunk, s3as, s3ar)
     afull[j] = chunk_of(0, j)
 
-    def forward(i):
+    def pair(c, pp):
+        return bop.at[pl.ds(2 * c, 2), pp]
+
+    def forward(c):
         @pl.loop(1, NX)
         def _(d):
-            send(bop.at[i, p], bop.at[i, p], s4bs.at[i, d], s4br.at[i, p], along_x((p + d) % NX))
-
-    forward(j)
-
-    @pl.loop(0, NP - 1)
+            send(pair(c, p), pair(c, p), s4bs.at[c, d], s4br.at[c, p], along_x((p + d) % NX))
+
+    other = j + 1 - 2 * (j % 2)
+    wait_for(bop.at[other, p], s3br.at[other])
+    forward(j // 2)
+
+    @pl.loop(0, CHIPS - 1)
     def _(n):
-        i = (j + NP - near_first(n)) % NP
-        wait_for(bop.at[i, p], s3br.at[i])
-        forward(i)
+        m = CHIPS - 2 - n
+        away = CHIPS // 2 + (m + 1) // 2 * (2 * (m % 2) - 1)
+        c = (j // 2 + CHIPS - away) % CHIPS
+        wait_for(bop.at[2 * c, p], s3br.at[2 * c])
+        wait_for(bop.at[2 * c + 1, p], s3br.at[2 * c + 1])
+        forward(c)
 
     wait_for(xv, x_sem)
 
@@ -274,9 +282,9 @@
         def _(d):
             pp = (p + d) % NX
 
-            @pl.loop(0, GC)
-            def _(n):
-                wait_for(bop.at[q * GC + n, pp], s4br.at[q * GC + n, pp])
+            @pl.loop(q * GC // 2, (q + 1) * GC // 2)
+            def _(c):
+                wait_for(pair(c, pp), s4br.at[c, pp])
 
         b_cols = side_by_side([bop[q * GC + n].reshape(NX * A, L) for n in range(GC)])
         x_cols = side_by_side([x_chunk(q * GC + n) for n in range(GC)])
@@ -466,9 +474,11 @@
                 wait_for(part.at[which, i], ps.at[0, which, i])
                 wait_for(part_s.at[which, i], ps.at[1, which, i])
 
+    @pl.loop(0, CHIPS)
+    def _(c):
         @pl.loop(1, NX)
         def _(d):
-            wait_for(bop.at[i, p], s4bs.at[i, d])
+            wait_for(pair(c, p), s4bs.at[c, d])
 
     @pl.loop(1, NX)
     def _(d):
@@ -549,7 +559,7 @@
             D((NP,)), D((NP,)),
             D((NP,)), D((NP,)),
             D((NX,)), D((NX,)),
-            D((NP, NX)), D((NP, NX)),
+            D((NP // 2, NX)), D((NP // 2, NX)),
             D((2, G, NX)), D((2, G, NX)),
             D((2, NX)), D((2, NX)),
             D((2, 2, NP)), D((2, 2, NP)),

time: 66.7 us -> 66.4 us (level)
  no operation moved by 1% of the time
where the time goes in v5:
time: 66.4 us; the launch traced here: 66.1 us
  Pallas kernels  64.7 us (97%)
  other arithmetic  1.38 us (2%)
    pallas_call x1, Pallas kernels, body(): pl.pallas_call(functools.partial(kernel, cfg), out_shape=jax.ShapeDtypeSt...  64.7 us
    mul x1, other arithmetic, body(): return 2.0 * (product - c_as.astype(F32))  1.38 us

profile of v5, /device:TPU:1, one launch (start us, length us, event | category | flops | bytes accessed | tf_op | source)
XLA Modules:
  0.0 66.1 jit_solution(8726181659253561265)
XLA Ops:
  0.0 0.0 copy-start
  0.0 64.7 %shard_map.55 = f32[32,240]{1,0:T(8,128)} custom-call(s32[2,120]{1,0:T(2,128)} %bitcast.1, s32[120]{0:T(128)} %slot_ref.1, bf16[32,240]{1,0:T(8,128)(2,1)} %r_ref.1, bf16[1,512,2048]{2,1,0:T(8,128)(2,1)} %x_hbm.1), custom_call_target="tpu_custom_call" | custom-call | tf_op jit(solution)/shard_map/pallas_call | solution.py:519
  64.8 0.0 copy-done
  64.8 1.4 %subtract_multiply_fusion = f32[32,240]{1,0:T(8,128)} fusion(f32[32,240]{1,0:T(8,128)} %shard_map.55, bf16[32,240]{1,0:T(8,128)(2,1)S(1)} %copy-done), kind=kLoop, calls=%fused_computation | loop fusion | flops 23040 | bytes 76800 | tf_op jit(solution)/shard_map/mul | solution.py:573
Async XLA Ops:
  0.0 64.8 %copy-start = (bf16[32,240]{1,0:T(8,128)(2,1)S(1)}, bf16[32,240]{1,0:T(8,128)(2,1)}, u32[]{:S(2)}) copy-start(bf16[32,240]{1,0:T(8,128)(2,1)} %param.6) | copy-start | bytes 46084
